TPU v7x, 32 devices: a whole 2x2x4 slice. The times are simulated.
32 devices in a mesh: dp: 2 (over core), glob: 4 (over y, x), byte: 4 (over z).
Axes of the slice: x: 2, y: 2, z: 4, core: 2. Of those that a mesh axis runs over, the one named last changes fastest.
Arguments:
- byte_states: bfloat16 [2, 512, 4096], P('dp', 'byte', 'glob'), may hold values from -8 to 8
- patch_start: int32 [2, 4, 32], P('dp'), may hold values from 0 to 128, as said below
- queries: bfloat16 [2, 128, 2048], P('dp', 'byte', 'glob'), may hold values from -6 to 6
- grad_out: bfloat16 [2, 128, 2048], P('dp', 'byte', 'glob'), may hold values from -6 to 6
- w_kv: bfloat16 [2, 4096, 512], P(None, 'byte', 'glob'), may hold values from -0.09375 to 0.09375
Outputs:
- attended: bfloat16 [2, 128, 2048], P('dp', 'byte', 'glob')
- grad_queries: bfloat16 [2, 128, 2048], P('dp', 'byte', 'glob')
- grad_bytes: bfloat16 [2, 512, 4096], P('dp', 'byte', 'glob')
- grad_kv: float32 [2, 4096, 512], P(None, 'byte', 'glob')
Inputs may be any that keep to these rules, and one draw needn't show every extreme that they name: Per shard: patch_start[s, 0] is 0, used slots come first with strictly rising starts, unused slots hold 128; a shard uses between 8 and 32 slots, and some shard of every draw uses all 32.
All inputs are finite; a program needn't handle non-finite values.
Results may differ from a plain program's by a relative error of at most 0.02.
Values may be sent and summed in bfloat16 or wider, within the bound.
A program may use at most 64 MiB of HBM per device.

v0:
```python
import math

import jax
import jax.numpy as jnp
from jax import lax
from jax.sharding import PartitionSpec as P

HS = 128


def segment_of(offsets, length):
    position = jnp.arange(length, dtype=jnp.int32)
    opened = (offsets[:, None] <= position[None, :]).astype(jnp.int32)
    return jnp.sum(opened, axis=0) - 1


def contract_rows(left, right):
    return lax.dot_general(
        left, right, (((0,), (0,)), ((), ())), preferred_element_type=jnp.float32
    )


def contract_cols(left, right):
    return lax.dot_general(
        left, right, (((1,), (1,)), ((), ())), preferred_element_type=jnp.float32
    )


def on_device(byte_states, patch_start, queries, grad_out, w_kv):
    states = byte_states[0]
    all_offsets = patch_start[0]
    cotangent = grad_out[0]
    byte_count = states.shape[0]
    shard_total = all_offsets.shape[0]
    slot_count = all_offsets.shape[1]
    slot_total = shard_total * slot_count
    shard = lax.axis_index("byte")
    offsets = lax.dynamic_index_in_dim(all_offsets, shard, 0, keepdims=False)
    head_count = cotangent.shape[1] // HS
    shared_heads = w_kv.shape[2] // HS
    group_size = head_count // shared_heads
    factor = 1.0 / math.sqrt(HS)
    segments = segment_of(offsets, byte_count)
    slot_range = jnp.arange(slot_count, dtype=jnp.int32)
    members = slot_range[:, None] == segments[None, :]
    counts = jnp.maximum(jnp.sum(members.astype(jnp.float32), axis=1), 1.0)
    summed = jnp.dot(members.astype(jnp.bfloat16), states, preferred_element_type=jnp.float32)
    pooled_part = (summed / counts[:, None]).astype(jnp.bfloat16)
    usable = all_offsets.reshape(slot_total) < byte_count
    live = lax.dynamic_slice_in_dim(usable, shard * slot_count, slot_count, 0)
    pair_full = lax.all_gather(w_kv, "byte", axis=1, tiled=True)
    pooled = lax.all_gather(pooled_part, "glob", axis=1, tiled=True)
    key_rows = jnp.dot(pooled, pair_full[0], preferred_element_type=jnp.float32).astype(
        jnp.bfloat16
    )
    value_rows = jnp.dot(pooled, pair_full[1], preferred_element_type=jnp.float32).astype(
        jnp.bfloat16
    )
    key_all, value_all = (
        lax.all_gather(key_rows, "byte", axis=0, tiled=True),
        lax.all_gather(value_rows, "byte", axis=0, tiled=True),
    )
    block_len = math.gcd(slot_total, 1024)
    block_total = slot_total // block_len
    key_blocks = key_all.reshape(block_total, block_len, shared_heads, HS)
    value_blocks = value_all.reshape(block_total, block_len, shared_heads, HS)
    id_blocks = jnp.arange(slot_total, dtype=jnp.int32).reshape(block_total, block_len)
    usable_blocks = usable.reshape(block_total, block_len)
    query_heads = queries[0].reshape(slot_count, shared_heads, group_size, HS)
    query_ids = shard * slot_count + slot_range
    live_rows = live.astype(jnp.bfloat16)[:, None, None, None]
    masked_grad = cotangent.reshape(slot_count, shared_heads, group_size, HS) * live_rows

    def scores_of(key_block, id_block, usable_block):
        scores = (
            jnp.einsum("qcgd,kcd->cgqk", query_heads, key_block, preferred_element_type=jnp.float32)
            * factor
        )
        visible = (id_block[None, :] <= query_ids[:, None]) & usable_block[None, :]
        return (jnp.where(visible, scores, -1e30), visible)

    def first_pass(carried, blocks):
        highest, totals = carried
        key_block, id_block, usable_block = blocks
        masked, visible = scores_of(key_block, id_block, usable_block)
        newest = jnp.maximum(highest, jnp.max(masked, axis=-1))
        raised = jnp.where(visible, jnp.exp(masked - newest[..., None]), 0.0)
        totals = totals * jnp.exp(highest - newest) + jnp.sum(raised, axis=-1)
        return ((newest, totals), None)

    start_high = jnp.full((shared_heads, group_size, slot_count), -1e30, jnp.float32)
    (highest, totals), unused = lax.scan(
        first_pass, (start_high, jnp.zeros_like(start_high)), (key_blocks, id_blocks, usable_blocks)
    )
    totals = jnp.maximum(totals, 1.0)

    def attention_of(masked, visible):
        raised = jnp.where(visible, jnp.exp(masked - highest[..., None]), 0.0)
        return raised / totals[..., None]

    def second_pass(mixed, blocks):
        key_block, value_block, id_block, usable_block = blocks
        masked, visible = scores_of(key_block, id_block, usable_block)
        shortened = attention_of(masked, visible).astype(jnp.bfloat16)
        return (
            mixed
            + jnp.einsum(
                "cgqk,kcd->qcgd", shortened, value_block, preferred_element_type=jnp.float32
            ),
            None,
        )

    zero_heads = jnp.zeros((slot_count, shared_heads, group_size, HS), jnp.float32)
    all_blocks = (key_blocks, value_blocks, id_blocks, usable_blocks)
    mixed, unused = lax.scan(second_pass, zero_heads, all_blocks)
    attended = (mixed * live.astype(jnp.float32)[:, None, None, None]).astype(jnp.bfloat16)
    attended = attended.reshape(1, slot_count, head_count * HS)
    row_dots = jnp.einsum("qcgd,qcgd->cgq", masked_grad.astype(jnp.float32), mixed)

    def third_pass(query_acc, blocks):
        key_block, value_block, id_block, usable_block = blocks
        masked, visible = scores_of(key_block, id_block, usable_block)
        attention = attention_of(masked, visible)
        shortened = attention.astype(jnp.bfloat16)
        prob_grad = jnp.einsum(
            "qcgd,kcd->cgqk", masked_grad, value_block, preferred_element_type=jnp.float32
        )
        score_grad = (attention * (prob_grad - row_dots[..., None]) * factor).astype(jnp.bfloat16)
        query_acc = query_acc + jnp.einsum(
            "cgqk,kcd->qcgd", score_grad, key_block, preferred_element_type=jnp.float32
        )
        key_part = jnp.einsum(
            "cgqk,qcgd->kcd", score_grad, query_heads, preferred_element_type=jnp.float32
        )
        value_part = jnp.einsum(
            "cgqk,qcgd->kcd", shortened, masked_grad, preferred_element_type=jnp.float32
        )
        return (query_acc, (key_part, value_part))

    query_acc, (key_parts, value_parts) = lax.scan(third_pass, zero_heads, all_blocks)
    query_grad = query_acc.astype(jnp.bfloat16).reshape(1, slot_count, head_count * HS)
    key_terms = key_parts.reshape(slot_total, shared_heads * HS)
    value_terms = value_parts.reshape(slot_total, shared_heads * HS)
    key_sum, value_sum = (
        lax.psum_scatter(
            key_terms.astype(jnp.bfloat16), "byte", scatter_dimension=0, tiled=True
        ).astype(jnp.float32),
        lax.psum_scatter(
            value_terms.astype(jnp.bfloat16), "byte", scatter_dimension=0, tiled=True
        ).astype(jnp.float32),
    )
    key_grad = key_sum.astype(jnp.bfloat16)
    value_grad = value_sum.astype(jnp.bfloat16)
    patch_part = contract_cols(key_grad, pair_full[0]) + contract_cols(value_grad, pair_full[1])
    patch_grad = lax.psum_scatter(
        patch_part.astype(jnp.bfloat16), "glob", scatter_dimension=1, tiled=True
    )
    pool_grad = patch_grad.astype(jnp.float32) / counts[:, None]
    byte_grad = jnp.take(pool_grad, segments, axis=0).astype(jnp.bfloat16)[None]
    key_value = jnp.concatenate([key_grad, value_grad], axis=1)
    pair_sum = lax.psum_scatter(
        contract_rows(pooled, key_value).astype(jnp.bfloat16),
        "byte",
        scatter_dimension=0,
        tiled=True,
    ).astype(jnp.float32)
    pair_sum = lax.psum(pair_sum.astype(jnp.bfloat16), "dp").astype(jnp.float32)
    pair_grad = pair_sum.reshape(pair_sum.shape[0], 2, shared_heads * HS).transpose(1, 0, 2)
    return (attended, query_grad, byte_grad, pair_grad)


def solution(mesh):
    placed = (
        P("dp", "byte", "glob"),
        P("dp", None, None),
        P("dp", "byte", "glob"),
        P("dp", "byte", "glob"),
        P(None, "byte", "glob"),
    )
    return jax.shard_map(
        on_device,
        mesh=mesh,
        in_specs=placed,
        out_specs=(
            P("dp", "byte", "glob"),
            P("dp", "byte", "glob"),
            P("dp", "byte", "glob"),
            P(None, "byte", "glob"),
        ),
        check_vma=False,
    )
```

profile of v0, /device:TPU:0, one launch (start us, length us, event | category | flops | bytes accessed | tf_op | source)
XLA Modules:
  0.0 229.4 jit_solution(9101778240431400211)
XLA Ops:
  7.2 0.0 copy-start
  7.2 0.0 all-gather.2.cloned.1.call-start
  7.2 0.7 all-gather.2.cloned.1.call-update
  7.9 0.0 reduce-scatter.5.cloned.1.call-start
  8.0 0.7 broadcast_compare_fusion
  8.7 0.1 lt.43
  8.7 0.8 reshape.183
  9.5 0.8 reshape_squeeze.2
  10.3 0.1 dynamic-slice_convert_fusion
  10.4 0.8 broadcast_multiply_fusion
  11.2 0.7 dynamic-slice_bitcast_fusion
  11.9 0.1 convert_reduce_fusion.1
  12.0 0.1 convert_reduce_fusion
  12.1 0.0 copy-done
  12.1 0.2 fusion.1
  12.3 10.4 %all_gather.12 = bf16[32,4096]{1,0:T(8,128)(2,1)S(1)} all-gather(bf16[32,1024]{1,0:T(8,128)(2,1)S(1)} %fusion.1), channel_id=1, replica_groups=mesh['dp'=2,'glob'=4,'byte'=4] {'glob'}, dimensions={1}, use_global_device_ids=true | all-gather | bytes 327680 | tf_op jit(solution)/shard_map/all_gather | solution.py:52
  22.8 0.1 fusion.36
  22.8 35.4 %all-gather.2.cloned.1.call-done = bf16[2,4096,128]{2,1,0:T(8,128)(2,1)} async-done(((bf16[2,1024,128]{2,1,0:T(8,128)(2,1)}), bf16[2,4096,128]{2,1,0:T(8,128)(2,1)}) %all-gather.2.cloned.1.call-update) | async-done | bytes 2097168 | tf_op jit(solution)/shard_map/all_gather | solution.py:51
  58.3 1.5 convolution_convert_fusion.2
  59.8 13.1 %all_gather.15 = bf16[128,128]{1,0:T(8,128)(2,1)S(1)} all-gather(bf16[32,128]{1,0:T(8,128)(2,1)S(1)} %convolution_convert_fusion.2), channel_id=1, replica_groups=mesh['dp'=2,'glob'=4,'byte'=4] {'byte'}, dimensions={0}, use_global_device_ids=true | all-gather | bytes 40960 | tf_op jit(solution)/shard_map/all_gather | solution.py:60
  72.9 0.2 fusion.42
  73.1 0.2 fusion.19
  73.3 1.5 convolution_convert_fusion.3
  74.8 13.1 %all_gather.14 = bf16[128,128]{1,0:T(8,128)(2,1)S(1)} all-gather(bf16[32,128]{1,0:T(8,128)(2,1)S(1)} %convolution_convert_fusion.3), channel_id=1, replica_groups=mesh['dp'=2,'glob'=4,'byte'=4] {'byte'}, dimensions={0}, use_global_device_ids=true | all-gather | bytes 40960 | tf_op jit(solution)/shard_map/all_gather | solution.py:61
  88.0 0.2 fusion.17
  88.2 0.2 fusion.16
  88.3 0.2 fusion.12
  88.5 0.8 fusion.7
  89.3 0.0 reduce-scatter.5.cloned.1.call-update
  89.3 0.0 reduce-scatter.7.cloned.1.call-start
  89.4 0.9 fusion.11
  90.3 0.0 reduce-scatter.7.cloned.1.call-update
  90.3 0.0 copy-start.1
  90.3 0.0 reduce-scatter.11.cloned.1.call-start
  90.4 16.8 %reduce-scatter.5.cloned.1.call-done = bf16[32,128]{1,0:T(8,128)(2,1)} async-done(((bf16[128,128]{1,0:T(8,128)(2,1)}), bf16[32,128]{1,0:T(8,128)(2,1)}) %reduce-scatter.5.cloned.1.call-update) | async-done | bytes 8208 | tf_op jit(solution)/shard_map/reduce_scatter | solution.py:145
  107.2 0.0 copy-start.2
  107.2 20.0 %reduce-scatter.7.cloned.1.call-done = bf16[32,128]{1,0:T(8,128)(2,1)} async-done(((bf16[128,128]{1,0:T(8,128)(2,1)}), bf16[32,128]{1,0:T(8,128)(2,1)}) %reduce-scatter.7.cloned.1.call-update) | async-done | bytes 8208 | tf_op jit(solution)/shard_map/reduce_scatter | solution.py:148
  127.2 2.8 %convolution_convert_fusion = bf16[4096,256]{1,0:T(8,128)(2,1)} fusion(bf16[32,4096]{1,0:T(8,128)(2,1)S(1)} %all_gather.12, bf16[32,128]{1,0:T(8,128)(2,1)} %reduce-scatter.7.cloned.1.call-done, bf16[32,128]{1,0:T(8,128)(2,1)} %reduce-scatter.5.cloned.1.call-done), kind=kOutput, calls=%fused_computation.1 | convolution fusion | flops 68190208 | bytes 2375680 | tf_op jit(solution)/shard_map/dot_general | solution.py:18
  130.0 0.0 copy-start.3
  130.0 0.0 reduce-scatter.11.cloned.1.call-update
  130.0 0.0 reduce-scatter.9.cloned.1.call-start
  130.1 0.0 copy-done.1
  130.1 0.0 copy-done.2
  130.1 0.4 fusion.13
  130.5 0.1 copy-done.3
  130.7 1.2 fusion
  131.8 0.0 reduce-scatter.9.cloned.1.call-update
  131.9 0.0 all-reduce.2.cloned.1.call-start
  132.0 0.6 reshape.185
  132.6 39.5 %reduce-scatter.11.cloned.1.call-done = bf16[1024,256]{1,0:T(8,128)(2,1)} async-done(((bf16[4096,256]{1,0:T(8,128)(2,1)}), bf16[1024,256]{1,0:T(8,128)(2,1)}) %reduce-scatter.11.cloned.1.call-update) | async-done | bytes 524304 | tf_op jit(solution)/shard_map/reduce_scatter | solution.py:161
  172.1 1.9 bitcast_bitcast_fusion
  174.1 0.0 all-reduce.2.cloned.1.call-update
  174.1 0.1 fusion.10
  174.3 0.6 reshape.188
  174.9 24.1 %reduce-scatter.9.cloned.1.call-done = bf16[32,1024]{1,0:T(8,128)(2,1)} async-done(((bf16[32,4096]{1,0:T(8,128)(2,1)}), bf16[32,1024]{1,0:T(8,128)(2,1)}) %reduce-scatter.9.cloned.1.call-update) | async-done | bytes 65552 | tf_op jit(solution)/shard_map/reduce_scatter | solution.py:155
  199.0 0.9 convert_divide_fusion
  199.9 0.9 gather_fusion
  200.8 0.8 fusion.14
  201.6 18.9 %all-reduce.2.cloned.1.call-done = bf16[2,1024,128]{2,1,0:T(8,128)(2,1)} async-done(((bf16[2,1024,128]{2,1,0:T(8,128)(2,1)}), bf16[2,1024,128]{2,1,0:T(8,128)(2,1)}) %all-reduce.2.cloned.1.call-update) | async-done | bytes 524304 | tf_op jit(solution)/shard_map/psum | solution.py:167
  220.5 2.1 transpose.53
  (11 shorter events, 0.1 us)
Async XLA Ops:
  7.2 5.0 %copy-start = (bf16[1,128,1024]{2,1,0:T(8,128)(2,1)S(1)}, bf16[1,128,1024]{2,1,0:T(8,128)(2,1)}, u32[]{:S(2)}) copy-start(bf16[1,128,1024]{2,1,0:T(8,128)(2,1)} %param.5) | copy-start | bytes 786436
  7.2 51.1 %all-gather.2.cloned.1.call-start = ((), (), s32[]{:S(2)}) async-start(), calls=%async_computation.4 | async-start | bytes 2621440 | tf_op jit(solution)/shard_map/all_gather | solution.py:51
  7.9 99.3 %reduce-scatter.5.cloned.1.call-start = ((), (), s32[]{:S(2)}) async-start(), calls=%async_computation.5 | async-start | bytes 40960 | tf_op jit(solution)/shard_map/reduce_scatter | solution.py:145
  89.3 37.8 %reduce-scatter.7.cloned.1.call-start = ((), (), s32[]{:S(2)}) async-start(), calls=%async_computation.6 | async-start | bytes 40960 | tf_op jit(solution)/shard_map/reduce_scatter | solution.py:148
  90.3 39.7 %copy-start.1 = (bf16[2,4096,128]{2,1,0:T(8,128)(2,1)S(1)}, bf16[2,4096,128]{2,1,0:T(8,128)(2,1)}, u32[]{:S(2)}) copy-start(bf16[2,4096,128]{2,1,0:T(8,128)(2,1)} %all-gather.2.cloned.1.call-done) | copy-start | bytes 6291460
  90.3 81.8 %reduce-scatter.11.cloned.1.call-start = ((), (), s32[]{:S(2)}) async-start(), calls=%async_computation.8 | async-start | bytes 2621440 | tf_op jit(solution)/shard_map/reduce_scatter | solution.py:161
  107.2 22.9 %copy-start.2 = (bf16[32,128]{1,0:T(8,128)(2,1)S(1)}, bf16[32,128]{1,0:T(8,128)(2,1)}, u32[]{:S(2)}) copy-start(bf16[32,128]{1,0:T(8,128)(2,1)} %reduce-scatter.5.cloned.1.call-done) | copy-start | bytes 24580
  130.0 0.7 copy-start.3
  130.0 69.0 %reduce-scatter.9.cloned.1.call-start = ((), (), s32[]{:S(2)}) async-start(), calls=%async_computation.7 | async-start | bytes 327680 | tf_op jit(solution)/shard_map/reduce_scatter | solution.py:155
  131.9 88.6 %all-reduce.2.cloned.1.call-start = ((), (), s32[]{:S(2)}) async-start(), calls=%async_computation.9 | async-start | bytes 1048576 | tf_op jit(solution)/shard_map/psum | solution.py:167
Sparse Core Ops, SparseCore 0:
  9.6 48.6 all-gather.1
  89.5 17.6 reduce-scatter.4
  110.1 17.0 reduce-scatter.6
  130.1 41.9 reduce-scatter.10
  175.5 23.4 reduce-scatter.8
  201.8 18.6 all-reduce.1
where the time goes:
time: 230 us; the launch traced here: 229 us
  waiting for transfers between devices  155 us (67%)
  blocking collectives  36.7 us (16%)
  between operations  14.3 us (6%)
  matrix products  10.1 us (4%)
  local copies, waits for them, and re-layouts  6.6 us (3%)
  other arithmetic  6.08 us (3%)
    reduce_scatter x1, waiting for transfers between devices, on_device(): lax.psum_scatter(contract_rows(pooled, key_value).astype(jnp.bfloat16), '...  39.5 us
    all_gather x1, waiting for transfers between devices, on_device(): pair_full = lax.all_gather(w_kv, 'byte', axis=1, tiled=True)  35.4 us
    reduce_scatter x1, waiting for transfers between devices, on_device(): lax.psum_scatter(patch_part.astype(jnp.bfloat16), 'glob', scatter_dimensi...  24.1 us
    reduce_scatter x1, waiting for transfers between devices, on_device(): lax.psum_scatter(value_terms.astype(jnp.bfloat16), 'byte', scatter_dimens...  20 us
    psum x1, waiting for transfers between devices, on_device(): pair_sum = lax.psum(pair_sum.astype(jnp.bfloat16), 'dp').astype(jnp.float32)  18.9 us
    reduce_scatter x1, waiting for transfers between devices, on_device(): lax.psum_scatter(key_terms.astype(jnp.bfloat16), 'byte', scatter_dimensio...  16.8 us
    all_gather x1, blocking collectives, on_device(): lax.all_gather(value_rows, 'byte', axis=0, tiled=True)  13.1 us
    all_gather x1, blocking collectives, on_device(): lax.all_gather(key_rows, 'byte', axis=0, tiled=True)  13.1 us
  transfers between devices with their start and end apart: 6, of which 6 were waited for; matrix products, arithmetic and copies ran while one was open for 6% of the time, Pallas kernels for 0%

commit v1 on v0

v1 whole, which is shorter than its diff:
```python
import functools
import math

import jax
import jax.numpy as jnp
from jax import lax
from jax.experimental import pallas as pl
from jax.experimental.pallas import tpu as pltpu
from jax.sharding import PartitionSpec as P

HS = 128
MESH = pl.DeviceIdType.MESH
F32 = jnp.float32
BF16 = jnp.bfloat16


def mm(left, right, a, b):
    return lax.dot_general(left, right, (((a,), (b,)), ((), ())), preferred_element_type=F32)


def kernel(nd, ng, nb, states_ref, start_ref, query_ref, cot_ref, w_ref,
           att_ref, gq_ref, gb_ref, gkv_ref,
           pooled, pool_all, kv_part, kv_recv, kv_all, dkv_part, dkv_recv, dkv_all, dpart, drecv,
           s1, r1, s2, r2, s3, r3, s4, r4, s5, r5, s6, r6, sd, rd):
    dp = lax.axis_index("dp")
    g = lax.axis_index("glob")
    b = lax.axis_index("byte")
    ratio = nb // ng
    owner = b // ratio
    piece = lax.rem(b, ratio)
    diagonal = g == owner
    byte_count = states_ref.shape[1]
    slots = start_ref.shape[2]
    total = nb * slots
    chunk = w_ref.shape[1]
    width = w_ref.shape[2]
    shared = width // HS
    group = query_ref.shape[2] // width
    factor = 1.0 / math.sqrt(HS)

    def remote(src, dst, send, recv, **where):
        return pltpu.make_async_remote_copy(
            src_ref=src, dst_ref=dst, send_sem=send, recv_sem=recv,
            device_id=where, device_id_type=MESH)

    def unless(cond, fn):
        pl.when(jnp.logical_not(cond))(fn)

    barrier = pltpu.get_barrier_semaphore()

    def greet(**where):
        pl.semaphore_signal(barrier, inc=1, device_id=where, device_id_type=MESH)

    for g2 in range(ng):
        for c in range(ratio):
            unless(diagonal & (g2 == g) & (c == piece),
                   lambda g2=g2, c=c: greet(glob=jnp.int32(g2), byte=g * ratio + c))
    for s in range(nb):
        unless(diagonal & (s == b), lambda s=s: greet(glob=owner, byte=jnp.int32(s)))
    for o in range(1, nb):
        greet(byte=lax.rem(b + o, nb))
    for o in range(1, nd):
        greet(dp=lax.rem(dp + o, nd))

    row = start_ref[0, pl.ds(b, 1), :]
    i0 = lax.broadcasted_iota(jnp.int32, (slots, slots), 0)
    i1 = lax.broadcasted_iota(jnp.int32, (slots, slots), 1)
    spread = jnp.broadcast_to(row, (slots, slots))
    first = jnp.sum(jnp.where(i0 == i1, spread, 0), axis=1, keepdims=True)
    after = jnp.sum(jnp.where(i0 + 1 == i1, spread, 0), axis=1, keepdims=True)
    slot_col = lax.broadcasted_iota(jnp.int32, (slots, 1), 0)
    after = jnp.where(slot_col == slots - 1, byte_count, after)
    position = lax.broadcasted_iota(jnp.int32, (slots, byte_count), 1)
    members = jnp.where((first <= position) & (position < after), 1.0, 0.0).astype(F32)
    counts = jnp.maximum(jnp.sum(members, axis=1, keepdims=True), 1.0)
    members = members.astype(BF16)
    for c in range(ratio):
        summed = mm(members, states_ref[0, :, c * chunk:(c + 1) * chunk], 1, 0)
        pooled[c] = (summed / counts).astype(BF16)

    pl.semaphore_wait(barrier, 2 * nb - 2 * jnp.where(diagonal, 1, 0) + nb - 1 + nd - 1)

    def pool_copy(g2, c):
        return remote(pooled.at[c], pool_all.at[dp, b], s1.at[g2 * ratio + c], r1.at[b],
                      glob=jnp.int32(g2), byte=g * ratio + c)

    for g2 in range(ng):
        for c in range(ratio):
            unless(diagonal & (g2 == g) & (c == piece), lambda g2=g2, c=c: pool_copy(g2, c).start())

    @pl.when(diagonal)
    def _():
        pool_all[dp, b] = pooled[piece]

    spots = lax.broadcasted_iota(jnp.int32, (slots, total), 1)
    tiles = jnp.where(lax.rem(spots, slots) == lax.broadcasted_iota(jnp.int32, (slots, total), 0), 1.0, 0.0)
    used = jnp.where(start_ref[0] < byte_count, 1.0, 0.0)
    used = mm(used.astype(BF16), tiles.astype(BF16), 1, 0)
    lane = lax.broadcasted_iota(jnp.int32, (nb, total), 1)
    shard_of = lax.broadcasted_iota(jnp.int32, (nb, total), 0)
    mine = (lane >= shard_of * slots) & (lane < (shard_of + 1) * slots)
    used = jnp.sum(jnp.where(mine, used, 0.0), axis=0, keepdims=True)
    live = jnp.where(first < byte_count, 1.0, 0.0)
    lives = jnp.concatenate([live] * group, axis=0)
    rows = group * slots
    ids = b * slots + lax.rem(lax.broadcasted_iota(jnp.int32, (rows, total), 0), slots)
    keys = lax.broadcasted_iota(jnp.int32, (rows, total), 1)
    visible = (keys <= ids) & (jnp.broadcast_to(used, (rows, total)) > 0.5)

    for s in range(nb):
        unless(diagonal & (s == b), lambda s=s: remote(
            pooled.at[0], pool_all.at[dp, s], s1.at[0], r1.at[s], byte=b).wait_recv())

    for o in range(1, nd):
        remote(pool_all.at[dp], pool_all.at[dp], sd.at[0, o], rd.at[0, dp], dp=lax.rem(dp + o, nd)).start()

    gathered = pool_all[dp].reshape(total, chunk)
    for j in range(2):
        kv_part[:, :, j * width:(j + 1) * width] = (
            mm(gathered, w_ref[j], 1, 0).astype(BF16).reshape(nb, slots, width))

    def reduce(part, recv, whole, sa, ra, sb, rb):
        for o in range(1, nb):
            peer = lax.rem(b + o, nb)
            remote(part.at[peer], recv.at[b], sa.at[o], ra.at[b], byte=peer).start()
        acc = part[b].astype(F32)
        for o in range(1, nb):
            peer = lax.rem(b + o, nb)
            remote(part.at[peer], recv.at[peer], sa.at[o], ra.at[peer], byte=peer).wait_recv()
            acc = acc + recv[peer].astype(F32)
        whole[b] = acc.astype(BF16)
        for o in range(1, nb):
            remote(whole.at[b], whole.at[b], sb.at[o], rb.at[b], byte=lax.rem(b + o, nb)).start()
        for o in range(1, nb):
            peer = lax.rem(b + o, nb)
            remote(whole.at[b], whole.at[peer], sb.at[o], rb.at[peer], byte=peer).wait_recv()

    def sent(part, whole, recv, sa, ra, sb, rb):
        for o in range(1, nb):
            peer = lax.rem(b + o, nb)
            remote(part.at[peer], recv.at[b], sa.at[o], ra.at[b], byte=peer).wait_send()
            remote(whole.at[b], whole.at[b], sb.at[o], rb.at[b], byte=peer).wait_send()

    reduce(kv_part, kv_recv, kv_all, s2, r2, s3, r3)

    for c in range(shared):
        k = kv_all[:, :, c * HS:(c + 1) * HS].reshape(total, HS)
        v = kv_all[:, :, width + c * HS:width + (c + 1) * HS].reshape(total, HS)
        cols = [slice((c * group + h) * HS, (c * group + h + 1) * HS) for h in range(group)]
        q = jnp.concatenate([query_ref[0, :, at] for at in cols], axis=0)
        gm = jnp.concatenate([cot_ref[0, :, at] for at in cols], axis=0).astype(F32) * lives
        gm16 = gm.astype(BF16)
        scores = jnp.where(visible, mm(q, k, 1, 1) * factor, -1e30)
        top = jnp.max(scores, axis=1, keepdims=True)
        raised = jnp.where(visible, jnp.exp(scores - top), 0.0)
        prob = raised / jnp.maximum(jnp.sum(raised, axis=1, keepdims=True), 1.0)
        pb = prob.astype(BF16)
        mixed = mm(pb, v, 1, 0)
        dots = jnp.sum(gm * mixed, axis=1, keepdims=True)
        ds = (prob * (mm(gm16, v, 1, 1) - dots) * factor).astype(BF16)
        dkv_part[:, :, c * HS:(c + 1) * HS] = mm(ds, q, 0, 0).astype(BF16).reshape(nb, slots, HS)
        dkv_part[:, :, width + c * HS:width + (c + 1) * HS] = (
            mm(pb, gm16, 0, 0).astype(BF16).reshape(nb, slots, HS))
        att = (mixed * lives).astype(BF16)
        gq = mm(ds, k, 1, 0).astype(BF16)
        for h in range(group):
            att_ref[0, :, cols[h]] = att[h * slots:(h + 1) * slots]
            gq_ref[0, :, cols[h]] = gq[h * slots:(h + 1) * slots]

    reduce(dkv_part, dkv_recv, dkv_all.at[dp], s4, r4, s5, r5)
    for o in range(1, nd):
        remote(dkv_all.at[dp], dkv_all.at[dp], sd.at[1, o], rd.at[1, dp], dp=lax.rem(dp + o, nd)).start()

    dkv = dkv_all[dp].reshape(total, 2 * width)
    terms = mm(dkv[:, :width], w_ref[0], 1, 1) + mm(dkv[:, width:], w_ref[1], 1, 1)
    dpart[...] = terms.astype(BF16).reshape(nb, slots, chunk)

    def patch_copy(s):
        return remote(dpart.at[s], drecv.at[g, piece], s6.at[s], r6.at[g, piece], glob=owner, byte=jnp.int32(s))

    for s in range(nb):
        unless(diagonal & (s == b), lambda s=s: patch_copy(s).start())

    @pl.when(diagonal)
    def _():
        drecv[g, piece] = dpart[b]

    for o in range(1, nd):
        other = lax.rem(dp + o, nd)
        remote(pool_all.at[dp], pool_all.at[other], sd.at[0, o], rd.at[0, other], dp=other).wait_recv()
        remote(dkv_all.at[dp], dkv_all.at[other], sd.at[1, o], rd.at[1, other], dp=other).wait_recv()
    both = dkv_all[...].reshape(nd * total, 2 * width)
    step = math.gcd(chunk, 256)
    for at in range(0, chunk, step):
        piece_of = pool_all[:, :, :, at:at + step].reshape(nd * total, step)
        product = mm(piece_of, both, 0, 0)
        for j in range(2):
            gkv_ref[j, at:at + step, :] = product[:, j * width:(j + 1) * width]

    for g2 in range(ng):
        for c in range(ratio):
            unless(diagonal & (g2 == g) & (c == piece), lambda g2=g2, c=c: remote(
                dpart.at[0], drecv.at[g2, c], s6.at[0], r6.at[g2, c], byte=b).wait_recv())
    for c in range(ratio):
        acc = drecv[0, c].astype(F32)
        for g2 in range(1, ng):
            acc = acc + drecv[g2, c].astype(F32)
        share = (acc.astype(BF16).astype(F32) / counts).astype(BF16)
        gb_ref[0, :, c * chunk:(c + 1) * chunk] = mm(members, share, 0, 0).astype(BF16)

    for g2 in range(ng):
        for c in range(ratio):
            unless(diagonal & (g2 == g) & (c == piece), lambda g2=g2, c=c: pool_copy(g2, c).wait_send())
    sent(kv_part, kv_all, kv_recv, s2, r2, s3, r3)
    sent(dkv_part, dkv_all.at[dp], dkv_recv, s4, r4, s5, r5)
    for s in range(nb):
        unless(diagonal & (s == b), lambda s=s: patch_copy(s).wait_send())
    for o in range(1, nd):
        other = lax.rem(dp + o, nd)
        remote(pool_all.at[dp], pool_all.at[dp], sd.at[0, o], rd.at[0, dp], dp=other).wait_send()
        remote(dkv_all.at[dp], dkv_all.at[dp], sd.at[1, o], rd.at[1, dp], dp=other).wait_send()


def on_device(nd, ng, nb, byte_states, patch_start, queries, grad_out, w_kv):
    slots = patch_start.shape[2]
    chunk, width = w_kv.shape[1], w_kv.shape[2]
    ratio = nb // ng
    dma = pltpu.SemaphoreType.DMA
    vmem = pl.BlockSpec(memory_space=pltpu.VMEM)
    return pl.pallas_call(
        functools.partial(kernel, nd, ng, nb),
        out_shape=(
            jax.ShapeDtypeStruct(queries.shape, BF16),
            jax.ShapeDtypeStruct(queries.shape, BF16),
            jax.ShapeDtypeStruct(byte_states.shape, BF16),
            jax.ShapeDtypeStruct(w_kv.shape, F32),
        ),
        in_specs=[vmem] * 5,
        out_specs=(vmem,) * 4,
        scratch_shapes=[
            pltpu.VMEM((ratio, slots, chunk), BF16),
            pltpu.VMEM((nd, nb, slots, chunk), BF16),
            pltpu.VMEM((nb, slots, 2 * width), BF16),
            pltpu.VMEM((nb, slots, 2 * width), BF16),
            pltpu.VMEM((nb, slots, 2 * width), BF16),
            pltpu.VMEM((nb, slots, 2 * width), BF16),
            pltpu.VMEM((nb, slots, 2 * width), BF16),
            pltpu.VMEM((nd, nb, slots, 2 * width), BF16),
            pltpu.VMEM((nb, slots, chunk), BF16),
            pltpu.VMEM((ng, ratio, slots, chunk), BF16),
            dma((nb,)), dma((nb,)), dma((nb,)), dma((nb,)), dma((nb,)), dma((nb,)),
            dma((nb,)), dma((nb,)), dma((nb,)), dma((nb,)), dma((nb,)), dma((ng, ratio)),
            dma((2, nd)), dma((2, nd)),
        ],
        compiler_params=pltpu.CompilerParams(
            collective_id=0, has_side_effects=True, vmem_limit_bytes=48 * 1024 * 1024),
    )(byte_states, patch_start, queries, grad_out, w_kv)


def solution(mesh):
    sizes = (mesh.shape["dp"], mesh.shape["glob"], mesh.shape["byte"])
    placed = (
        P("dp", "byte", "glob"),
        P("dp", None, None),
        P("dp", "byte", "glob"),
        P("dp", "byte", "glob"),
        P(None, "byte", "glob"),
    )
    return jax.shard_map(
        functools.partial(on_device, *sizes),
        mesh=mesh,
        in_specs=placed,
        out_specs=(
            P("dp", "byte", "glob"),
            P("dp", "byte", "glob"),
            P("dp", "byte", "glob"),
            P(None, "byte", "glob"),
        ),
        check_vma=False,
    )
```

time: 230 us -> 55.6 us (0.24)
  waiting for transfers between devices: 155 us -> 0 us
  Pallas kernels: 0 us -> 47.5 us
  blocking collectives: 36.7 us -> 0 us
  between operations: 14.3 us -> 0.65 us
  matrix products: 10.1 us -> 0 us
  other arithmetic: 6.08 us -> 0 us
    reduce_scatter x4 -> x0, waiting for transfers between devices: 100 us -> none  [the longest x1 39.5 us: on_device(): lax.psum_scatter(contract_rows(pooled, key_value).astype(jnp.bfloat16), '...]
    pallas_call x0 -> x1, Pallas kernels: none -> 47.5 us  [on_device(): pl.pallas_call(functools.partial(kernel, nd, ng, nb), out_shape=(jax.Shap...]
    all_gather x3 -> x0, blocking collectives: 36.7 us -> none  [the longest x1 13.1 us: on_device(): lax.all_gather(value_rows, 'byte', axis=0, tiled=True)]
    all_gather x1 -> x0, waiting for transfers between devices: 35.4 us -> none  [on_device(): pair_full = lax.all_gather(w_kv, 'byte', axis=1, tiled=True)]
    psum x1 -> x0, waiting for transfers between devices: 18.9 us -> none  [on_device(): pair_sum = lax.psum(pair_sum.astype(jnp.bfloat16), 'dp').astype(jnp.float32)]
    dot_general x12 -> x0, matrix products: 10.1 us -> none  [the longest x1 2.82 us: contract_rows(): lax.dot_general(left, right, (((0,), (0,)), ((), ())), preferred_element_...]
    unnamed x8 -> x14, local copies, waits for them, and re-layouts: 0.16 us -> 7.08 us
  transfers between devices with their start and end apart: 6 -> 0, of which waited for: 6 -> 0; matrix products, arithmetic and copies ran while one was open for 6% -> 0% of each run, Pallas kernels for 0% -> 0%
where the time goes in v1:
time: 55.6 us; the launch traced here: 55.2 us
  Pallas kernels  47.5 us (85%)
  local copies, waits for them, and re-layouts  7.08 us (13%)
  between operations  0.65 us (1%)
    pallas_call x1, Pallas kernels, on_device(): pl.pallas_call(functools.partial(kernel, nd, ng, nb), out_shape=(jax.Shap...  47.5 us
    unnamed x14, local copies, waits for them, and re-layouts  7.08 us

profile of v1, /device:TPU:0, one launch (start us, length us, event | category | flops | bytes accessed | tf_op | source)
XLA Modules:
  0.0 55.2 jit_solution(7895387509932076976)
XLA Ops:
  0.6 0.0 copy-start
  0.6 1.0 %copy-done = bf16[2,1024,128]{2,1,0:T(8,128)(2,1)S(1)} copy-done((bf16[2,1024,128]{2,1,0:T(8,128)(2,1)S(1)}, bf16[2,1024,128]{2,1,0:T(8,128)(2,1)}, u32[]{:S(2)}) %copy-start) | copy-done | bytes 524312
  1.7 0.0 copy-start.1
  1.7 0.9 %copy-done.1 = bf16[1,128,1024]{2,1,0:T(8,128)(2,1)S(1)} copy-done((bf16[1,128,1024]{2,1,0:T(8,128)(2,1)S(1)}, bf16[1,128,1024]{2,1,0:T(8,128)(2,1)}, u32[]{:S(2)}) %copy-start.1) | copy-done | bytes 262168
  2.6 0.0 copy-start.2
  2.6 0.8 %copy-done.2 = bf16[1,32,512]{2,1,0:T(8,128)(2,1)S(1)} copy-done((bf16[1,32,512]{2,1,0:T(8,128)(2,1)S(1)}, bf16[1,32,512]{2,1,0:T(8,128)(2,1)}, u32[]{:S(2)}) %copy-start.2) | copy-done | bytes 32792
  3.4 0.0 copy-start.3
  3.4 0.8 %copy-done.3 = bf16[1,32,512]{2,1,0:T(8,128)(2,1)S(1)} copy-done((bf16[1,32,512]{2,1,0:T(8,128)(2,1)S(1)}, bf16[1,32,512]{2,1,0:T(8,128)(2,1)}, u32[]{:S(2)}) %copy-start.3) | copy-done | bytes 32792
  4.1 0.0 copy-start.4
  4.1 0.7 %copy-done.4 = s32[1,4,32]{2,1,0:T(4,128)S(1)} copy-done((s32[1,4,32]{2,1,0:T(4,128)S(1)}, s32[1,4,32]{2,1,0:T(4,128)}, u32[]{:S(2)}) %copy-start.4) | copy-done | bytes 536
  4.8 47.5 %shard_map.84 = (bf16[1,32,512]{2,1,0:T(8,128)(2,1)S(1)}, bf16[1,32,512]{2,1,0:T(8,128)(2,1)S(1)}, bf16[1,128,1024]{2,1,0:T(8,128)(2,1)S(1)}, f32[2,1024,128]{2,1,0:T(8,128)S(1)}) custom-call(bf16[1,128,1024]{2,1,0:T(8,128)(2,1)S(1)} %copy-done.1, s32[1,4,32]{2,1,0:T(4,128)S(1)} %copy-done.4, bf16[1,32,512]{2,1,0:T(8,128)(2,1)S(1)} %copy-done.2, ...), custom_call_target="tpu_custom_call" | custom-call | tf_op jit(solution)/shard_map/pallas_call | solution.py:230
  52.3 0.6 %copy.13 = bf16[1,32,512]{2,1,0:T(8,128)(2,1)} copy(bf16[1,32,512]{2,1,0:T(8,128)(2,1)S(1)} %get-tuple-element.8) | data formatting | bytes 65536
  53.0 0.6 %copy.14 = bf16[1,32,512]{2,1,0:T(8,128)(2,1)} copy(bf16[1,32,512]{2,1,0:T(8,128)(2,1)S(1)} %get-tuple-element.9) | data formatting | bytes 65536
  53.6 0.7 %copy.15 = bf16[1,128,1024]{2,1,0:T(8,128)(2,1)} copy(bf16[1,128,1024]{2,1,0:T(8,128)(2,1)S(1)} %get-tuple-element.10) | data formatting | bytes 524288
  54.3 1.0 %copy.16 = f32[2,1024,128]{2,1,0:T(8,128)} copy(f32[2,1024,128]{2,1,0:T(8,128)S(1)} %get-tuple-element.11) | data formatting | bytes 2097152
Async XLA Ops:
  0.6 1.0 %copy-start = (bf16[2,1024,128]{2,1,0:T(8,128)(2,1)S(1)}, bf16[2,1024,128]{2,1,0:T(8,128)(2,1)}, u32[]{:S(2)}) copy-start(bf16[2,1024,128]{2,1,0:T(8,128)(2,1)} %w_ref.1) | copy-start | bytes 1572868
  1.7 0.9 %copy-start.1 = (bf16[1,128,1024]{2,1,0:T(8,128)(2,1)S(1)}, bf16[1,128,1024]{2,1,0:T(8,128)(2,1)}, u32[]{:S(2)}) copy-start(bf16[1,128,1024]{2,1,0:T(8,128)(2,1)} %states_ref.1) | copy-start | bytes 786436
  2.6 0.8 %copy-start.2 = (bf16[1,32,512]{2,1,0:T(8,128)(2,1)S(1)}, bf16[1,32,512]{2,1,0:T(8,128)(2,1)}, u32[]{:S(2)}) copy-start(bf16[1,32,512]{2,1,0:T(8,128)(2,1)} %query_ref.1) | copy-start | bytes 98308
  3.4 0.8 %copy-start.3 = (bf16[1,32,512]{2,1,0:T(8,128)(2,1)S(1)}, bf16[1,32,512]{2,1,0:T(8,128)(2,1)}, u32[]{:S(2)}) copy-start(bf16[1,32,512]{2,1,0:T(8,128)(2,1)} %cot_ref.1) | copy-start | bytes 98308
  4.1 0.7 %copy-start.4 = (s32[1,4,32]{2,1,0:T(4,128)S(1)}, s32[1,4,32]{2,1,0:T(4,128)}, u32[]{:S(2)}) copy-start(s32[1,4,32]{2,1,0:T(4,128)} %start_ref.1) | copy-start | bytes 1540

commit v2 on v1

--- a/solution.py
+++ b/solution.py
@@ -18,10 +18,16 @@
     return lax.dot_general(left, right, (((a,), (b,)), ((), ())), preferred_element_type=F32)
 
 
-def kernel(nd, ng, nb, states_ref, start_ref, query_ref, cot_ref, w_ref,
+def kernel(nd, ng, nb, states_hbm, start_hbm, query_hbm, cot_hbm, w_hbm,
            att_ref, gq_ref, gb_ref, gkv_ref,
-           pooled, pool_all, kv_part, kv_recv, kv_all, dkv_part, dkv_recv, dkv_all, dpart, drecv,
-           s1, r1, s2, r2, s3, r3, s4, r4, s5, r5, s6, r6, sd, rd):
+           states_ref, start_ref, query_ref, cot_ref, w_ref, loads,
+           pooled, quarter, pool_all, kv_part, kv_recv, kv_all, dkv_part, dkv_recv, dkv_all, dpart, dterm, dsum, drecv,
+           s0, r0, s7, r7, s1, r1, s2, r2, s3, r3, s4, r4, s5, r5, s6, r6, sd, rd):
+    fetch = [pltpu.make_async_copy(src, dst, loads.at[at]) for at, (src, dst) in enumerate((
+        (start_hbm, start_ref), (states_hbm, states_ref), (w_hbm, w_ref),
+        (query_hbm, query_ref), (cot_hbm, cot_ref)))]
+    for load in fetch:
+        load.start()
     dp = lax.axis_index("dp")
     g = lax.axis_index("glob")
     b = lax.axis_index("byte")
@@ -35,6 +41,7 @@
     chunk = w_ref.shape[1]
     width = w_ref.shape[2]
     shared = width // HS
+    part = chunk // ng
     group = query_ref.shape[2] // width
     factor = 1.0 / math.sqrt(HS)
 
@@ -59,8 +66,12 @@
         unless(diagonal & (s == b), lambda s=s: greet(glob=owner, byte=jnp.int32(s)))
     for o in range(1, nb):
         greet(byte=lax.rem(b + o, nb))
+    for o in range(1, ng):
+        greet(glob=lax.rem(g + o, ng))
     for o in range(1, nd):
         greet(dp=lax.rem(dp + o, nd))
+    fetch[0].wait()
+    fetch[1].wait()
 
     row = start_ref[0, pl.ds(b, 1), :]
     i0 = lax.broadcasted_iota(jnp.int32, (slots, slots), 0)
@@ -76,12 +87,14 @@
     members = members.astype(BF16)
     for c in range(ratio):
         summed = mm(members, states_ref[0, :, c * chunk:(c + 1) * chunk], 1, 0)
-        pooled[c] = (summed / counts).astype(BF16)
-
-    pl.semaphore_wait(barrier, 2 * nb - 2 * jnp.where(diagonal, 1, 0) + nb - 1 + nd - 1)
+        means = (summed / counts).astype(BF16)
+        for i in range(ng):
+            pooled[c, i] = means[:, i * part:(i + 1) * part]
+
+    pl.semaphore_wait(barrier, 2 * nb - 2 * jnp.where(diagonal, 1, 0) + nb - 1 + ng - 1 + nd - 1)
 
     def pool_copy(g2, c):
-        return remote(pooled.at[c], pool_all.at[dp, b], s1.at[g2 * ratio + c], r1.at[b],
+        return remote(pooled.at[c, g2], quarter.at[b], s1.at[g2 * ratio + c], r1.at[b],
                       glob=jnp.int32(g2), byte=g * ratio + c)
 
     for g2 in range(ng):
@@ -90,7 +103,7 @@
 
     @pl.when(diagonal)
     def _():
-        pool_all[dp, b] = pooled[piece]
+        quarter[b] = pooled[piece, g]
 
     spots = lax.broadcasted_iota(jnp.int32, (slots, total), 1)
     tiles = jnp.where(lax.rem(spots, slots) == lax.broadcasted_iota(jnp.int32, (slots, total), 0), 1.0, 0.0)
@@ -109,15 +122,28 @@
 
     for s in range(nb):
         unless(diagonal & (s == b), lambda s=s: remote(
-            pooled.at[0], pool_all.at[dp, s], s1.at[0], r1.at[s], byte=b).wait_recv())
+            pooled.at[0, 0], quarter.at[s], s1.at[0], r1.at[s], byte=b).wait_recv())
+
+    def plane_copy(o, slot):
+        return remote(quarter, pool_all.at[dp, slot], s0.at[o], r0.at[slot], glob=lax.rem(g + o, ng))
+
+    for o in range(1, ng):
+        plane_copy(o, g).start()
+    pool_all[dp, g] = quarter[...]
+    fetch[2].wait()
+    for o in range(1, ng):
+        plane_copy(o, lax.rem(g + o, ng)).wait_recv()
 
     for o in range(1, nd):
         remote(pool_all.at[dp], pool_all.at[dp], sd.at[0, o], rd.at[0, dp], dp=lax.rem(dp + o, nd)).start()
 
-    gathered = pool_all[dp].reshape(total, chunk)
     for j in range(2):
-        kv_part[:, :, j * width:(j + 1) * width] = (
-            mm(gathered, w_ref[j], 1, 0).astype(BF16).reshape(nb, slots, width))
+        acc = mm(pool_all[dp, 0].reshape(total, part), w_ref[j, :part], 1, 0)
+        for i in range(1, ng):
+            acc = acc + mm(pool_all[dp, i].reshape(total, part), w_ref[j, i * part:(i + 1) * part], 1, 0)
+        kv_part[:, :, j * width:(j + 1) * width] = acc.astype(BF16).reshape(nb, slots, width)
+    fetch[3].wait()
+    fetch[4].wait()
 
     def reduce(part, recv, whole, sa, ra, sb, rb):
         for o in range(1, nb):
@@ -173,46 +199,61 @@
 
     dkv = dkv_all[dp].reshape(total, 2 * width)
     terms = mm(dkv[:, :width], w_ref[0], 1, 1) + mm(dkv[:, width:], w_ref[1], 1, 1)
-    dpart[...] = terms.astype(BF16).reshape(nb, slots, chunk)
-
-    def patch_copy(s):
-        return remote(dpart.at[s], drecv.at[g, piece], s6.at[s], r6.at[g, piece], glob=owner, byte=jnp.int32(s))
-
-    for s in range(nb):
-        unless(diagonal & (s == b), lambda s=s: patch_copy(s).start())
-
-    @pl.when(diagonal)
-    def _():
-        drecv[g, piece] = dpart[b]
+    for i in range(ng):
+        dpart[i] = terms[:, i * part:(i + 1) * part].astype(BF16).reshape(nb, slots, part)
+
+    def cut_copy(o, slot):
+        peer = lax.rem(g + o, ng)
+        return remote(dpart.at[peer], dterm.at[slot], s7.at[o], r7.at[slot], glob=peer)
+
+    for o in range(1, ng):
+        cut_copy(o, g).start()
 
     for o in range(1, nd):
         other = lax.rem(dp + o, nd)
         remote(pool_all.at[dp], pool_all.at[other], sd.at[0, o], rd.at[0, other], dp=other).wait_recv()
         remote(dkv_all.at[dp], dkv_all.at[other], sd.at[1, o], rd.at[1, other], dp=other).wait_recv()
     both = dkv_all[...].reshape(nd * total, 2 * width)
-    step = math.gcd(chunk, 256)
-    for at in range(0, chunk, step):
-        piece_of = pool_all[:, :, :, at:at + step].reshape(nd * total, step)
-        product = mm(piece_of, both, 0, 0)
+    for i in range(ng):
+        product = mm(pool_all[:, i].reshape(nd * total, part), both, 0, 0)
         for j in range(2):
-            gkv_ref[j, at:at + step, :] = product[:, j * width:(j + 1) * width]
+            gkv_ref[j, i * part:(i + 1) * part, :] = product[:, j * width:(j + 1) * width]
+
+    acc = dpart[g].astype(F32)
+    for o in range(1, ng):
+        peer = lax.rem(g + o, ng)
+        cut_copy(o, peer).wait_recv()
+        acc = acc + dterm[peer].astype(F32)
+    dsum[...] = acc.astype(BF16)
+
+    def patch_copy(s):
+        return remote(dsum.at[s], drecv.at[g, piece], s6.at[s], r6.at[g, piece], glob=owner, byte=jnp.int32(s))
+
+    for s in range(nb):
+        unless(diagonal & (s == b), lambda s=s: patch_copy(s).start())
+
+    @pl.when(diagonal)
+    def _():
+        drecv[g, piece] = dsum[b]
 
     for g2 in range(ng):
         for c in range(ratio):
             unless(diagonal & (g2 == g) & (c == piece), lambda g2=g2, c=c: remote(
-                dpart.at[0], drecv.at[g2, c], s6.at[0], r6.at[g2, c], byte=b).wait_recv())
+                dsum.at[0], drecv.at[g2, c], s6.at[0], r6.at[g2, c], byte=b).wait_recv())
     for c in range(ratio):
-        acc = drecv[0, c].astype(F32)
-        for g2 in range(1, ng):
-            acc = acc + drecv[g2, c].astype(F32)
-        share = (acc.astype(BF16).astype(F32) / counts).astype(BF16)
-        gb_ref[0, :, c * chunk:(c + 1) * chunk] = mm(members, share, 0, 0).astype(BF16)
+        for i in range(ng):
+            share = (drecv[i, c].astype(F32) / counts).astype(BF16)
+            first_col = c * chunk + i * part
+            gb_ref[0, :, first_col:first_col + part] = mm(members, share, 0, 0).astype(BF16)
 
     for g2 in range(ng):
         for c in range(ratio):
             unless(diagonal & (g2 == g) & (c == piece), lambda g2=g2, c=c: pool_copy(g2, c).wait_send())
     sent(kv_part, kv_all, kv_recv, s2, r2, s3, r3)
     sent(dkv_part, dkv_all.at[dp], dkv_recv, s4, r4, s5, r5)
+    for o in range(1, ng):
+        plane_copy(o, g).wait_send()
+        cut_copy(o, g).wait_send()
     for s in range(nb):
         unless(diagonal & (s == b), lambda s=s: patch_copy(s).wait_send())
     for o in range(1, nd):
@@ -225,6 +266,7 @@
     slots = patch_start.shape[2]
     chunk, width = w_kv.shape[1], w_kv.shape[2]
     ratio = nb // ng
+    part = chunk // ng
     dma = pltpu.SemaphoreType.DMA
     vmem = pl.BlockSpec(memory_space=pltpu.VMEM)
     return pl.pallas_call(
@@ -235,19 +277,29 @@
             jax.ShapeDtypeStruct(byte_states.shape, BF16),
             jax.ShapeDtypeStruct(w_kv.shape, F32),
         ),
-        in_specs=[vmem] * 5,
+        in_specs=[pl.BlockSpec(memory_space=pltpu.HBM)] * 5,
         out_specs=(vmem,) * 4,
         scratch_shapes=[
-            pltpu.VMEM((ratio, slots, chunk), BF16),
-            pltpu.VMEM((nd, nb, slots, chunk), BF16),
+            pltpu.VMEM(byte_states.shape, BF16),
+            pltpu.VMEM(patch_start.shape, patch_start.dtype),
+            pltpu.VMEM(queries.shape, BF16),
+            pltpu.VMEM(grad_out.shape, BF16),
+            pltpu.VMEM(w_kv.shape, BF16),
+            dma((5,)),
+            pltpu.VMEM((ratio, ng, slots, part), BF16),
+            pltpu.VMEM((nb, slots, part), BF16),
+            pltpu.VMEM((nd, ng, nb, slots, part), BF16),
             pltpu.VMEM((nb, slots, 2 * width), BF16),
             pltpu.VMEM((nb, slots, 2 * width), BF16),
             pltpu.VMEM((nb, slots, 2 * width), BF16),
             pltpu.VMEM((nb, slots, 2 * width), BF16),
             pltpu.VMEM((nb, slots, 2 * width), BF16),
             pltpu.VMEM((nd, nb, slots, 2 * width), BF16),
-            pltpu.VMEM((nb, slots, chunk), BF16),
-            pltpu.VMEM((ng, ratio, slots, chunk), BF16),
+            pltpu.VMEM((ng, nb, slots, part), BF16),
+            pltpu.VMEM((ng, nb, slots, part), BF16),
+            pltpu.VMEM((nb, slots, part), BF16),
+            pltpu.VMEM((ng, ratio, slots, part), BF16),
+            dma((ng,)), dma((ng,)), dma((ng,)), dma((ng,)),
             dma((nb,)), dma((nb,)), dma((nb,)), dma((nb,)), dma((nb,)), dma((nb,)),
             dma((nb,)), dma((nb,)), dma((nb,)), dma((nb,)), dma((nb,)), dma((ng, ratio)),
             dma((2, nd)), dma((2, nd)),

time: 55.6 us -> 49.7 us (0.89)
  Pallas kernels: 47.5 us -> 41.6 us
    pallas_call x1, Pallas kernels: 47.5 us -> 41.6 us  [on_device(): pl.pallas_call(functools.partial(kernel, nd, ng, nb), out_shape=(jax.Shap...]
where the time goes in v2:
time: 49.7 us; the launch traced here: 49.3 us
  Pallas kernels  41.6 us (84%)
  local copies, waits for them, and re-layouts  7.08 us (14%)
  between operations  0.65 us (1%)
    pallas_call x1, Pallas kernels, on_device(): pl.pallas_call(functools.partial(kernel, nd, ng, nb), out_shape=(jax.Shap...  41.6 us
    unnamed x14, local copies, waits for them, and re-layouts  7.08 us

profile of v2, /device:TPU:0, one launch (start us, length us, event | category | flops | bytes accessed | tf_op | source)
XLA Modules:
  0.0 49.3 jit_solution(10298819882822588689)
XLA Ops:
  0.6 0.0 copy-start
  0.6 1.0 %copy-done = bf16[2,1024,128]{2,1,0:T(8,128)(2,1)S(1)} copy-done((bf16[2,1024,128]{2,1,0:T(8,128)(2,1)S(1)}, bf16[2,1024,128]{2,1,0:T(8,128)(2,1)}, u32[]{:S(2)}) %copy-start) | copy-done | bytes 524312
  1.7 0.0 copy-start.1
  1.7 0.9 %copy-done.1 = bf16[1,128,1024]{2,1,0:T(8,128)(2,1)S(1)} copy-done((bf16[1,128,1024]{2,1,0:T(8,128)(2,1)S(1)}, bf16[1,128,1024]{2,1,0:T(8,128)(2,1)}, u32[]{:S(2)}) %copy-start.1) | copy-done | bytes 262168
  2.6 0.0 copy-start.2
  2.6 0.8 %copy-done.2 = bf16[1,32,512]{2,1,0:T(8,128)(2,1)S(1)} copy-done((bf16[1,32,512]{2,1,0:T(8,128)(2,1)S(1)}, bf16[1,32,512]{2,1,0:T(8,128)(2,1)}, u32[]{:S(2)}) %copy-start.2) | copy-done | bytes 32792
  3.4 0.0 copy-start.3
  3.4 0.8 %copy-done.3 = bf16[1,32,512]{2,1,0:T(8,128)(2,1)S(1)} copy-done((bf16[1,32,512]{2,1,0:T(8,128)(2,1)S(1)}, bf16[1,32,512]{2,1,0:T(8,128)(2,1)}, u32[]{:S(2)}) %copy-start.3) | copy-done | bytes 32792
  4.1 0.0 copy-start.4
  4.1 0.7 %copy-done.4 = s32[1,4,32]{2,1,0:T(4,128)S(1)} copy-done((s32[1,4,32]{2,1,0:T(4,128)S(1)}, s32[1,4,32]{2,1,0:T(4,128)}, u32[]{:S(2)}) %copy-start.4) | copy-done | bytes 536
  4.8 41.6 %shard_map.84 = (bf16[1,32,512]{2,1,0:T(8,128)(2,1)S(1)}, bf16[1,32,512]{2,1,0:T(8,128)(2,1)S(1)}, bf16[1,128,1024]{2,1,0:T(8,128)(2,1)S(1)}, f32[2,1024,128]{2,1,0:T(8,128)S(1)}) custom-call(bf16[1,128,1024]{2,1,0:T(8,128)(2,1)S(1)} %copy-done.1, s32[1,4,32]{2,1,0:T(4,128)S(1)} %copy-done.4, bf16[1,32,512]{2,1,0:T(8,128)(2,1)S(1)} %copy-done.2, ...), custom_call_target="tpu_custom_call" | custom-call | tf_op jit(solution)/shard_map/pallas_call | solution.py:272
  46.4 0.6 %copy.13 = bf16[1,32,512]{2,1,0:T(8,128)(2,1)} copy(bf16[1,32,512]{2,1,0:T(8,128)(2,1)S(1)} %get-tuple-element.8) | data formatting | bytes 65536
  47.0 0.6 %copy.14 = bf16[1,32,512]{2,1,0:T(8,128)(2,1)} copy(bf16[1,32,512]{2,1,0:T(8,128)(2,1)S(1)} %get-tuple-element.9) | data formatting | bytes 65536
  47.6 0.7 %copy.15 = bf16[1,128,1024]{2,1,0:T(8,128)(2,1)} copy(bf16[1,128,1024]{2,1,0:T(8,128)(2,1)S(1)} %get-tuple-element.10) | data formatting | bytes 524288
  48.3 1.0 %copy.16 = f32[2,1024,128]{2,1,0:T(8,128)} copy(f32[2,1024,128]{2,1,0:T(8,128)S(1)} %get-tuple-element.11) | data formatting | bytes 2097152
Async XLA Ops:
  0.6 1.0 %copy-start = (bf16[2,1024,128]{2,1,0:T(8,128)(2,1)S(1)}, bf16[2,1024,128]{2,1,0:T(8,128)(2,1)}, u32[]{:S(2)}) copy-start(bf16[2,1024,128]{2,1,0:T(8,128)(2,1)} %w_hbm.1) | copy-start | bytes 1572868
  1.7 0.9 %copy-start.1 = (bf16[1,128,1024]{2,1,0:T(8,128)(2,1)S(1)}, bf16[1,128,1024]{2,1,0:T(8,128)(2,1)}, u32[]{:S(2)}) copy-start(bf16[1,128,1024]{2,1,0:T(8,128)(2,1)} %states_hbm.1) | copy-start | bytes 786436
  2.6 0.8 %copy-start.2 = (bf16[1,32,512]{2,1,0:T(8,128)(2,1)S(1)}, bf16[1,32,512]{2,1,0:T(8,128)(2,1)}, u32[]{:S(2)}) copy-start(bf16[1,32,512]{2,1,0:T(8,128)(2,1)} %query_hbm.1) | copy-start | bytes 98308
  3.4 0.8 %copy-start.3 = (bf16[1,32,512]{2,1,0:T(8,128)(2,1)S(1)}, bf16[1,32,512]{2,1,0:T(8,128)(2,1)}, u32[]{:S(2)}) copy-start(bf16[1,32,512]{2,1,0:T(8,128)(2,1)} %cot_hbm.1) | copy-start | bytes 98308
  4.1 0.7 %copy-start.4 = (s32[1,4,32]{2,1,0:T(4,128)S(1)}, s32[1,4,32]{2,1,0:T(4,128)}, u32[]{:S(2)}) copy-start(s32[1,4,32]{2,1,0:T(4,128)} %start_hbm.1) | copy-start | bytes 1540

commit v3 on v2

--- a/solution.py
+++ b/solution.py
@@ -19,13 +19,17 @@
 
 
 def kernel(nd, ng, nb, states_hbm, start_hbm, query_hbm, cot_hbm, w_hbm,
-           att_ref, gq_ref, gb_ref, gkv_ref,
-           states_ref, start_ref, query_ref, cot_ref, w_ref, loads,
+           att_hbm, gq_hbm, gb_hbm, gkv_hbm,
+           states_ref, start_ref, query_ref, cot_ref, w_ref, wt_ref, loads,
+           att_ref, gq_ref, gb_ref, gkv_ref, stores,
            pooled, quarter, pool_all, kv_part, kv_recv, kv_all, dkv_part, dkv_recv, dkv_all, dpart, dterm, dsum, drecv,
            s0, r0, s7, r7, s1, r1, s2, r2, s3, r3, s4, r4, s5, r5, s6, r6, sd, rd):
     fetch = [pltpu.make_async_copy(src, dst, loads.at[at]) for at, (src, dst) in enumerate((
-        (start_hbm, start_ref), (states_hbm, states_ref), (w_hbm, w_ref),
+        (start_hbm, start_ref), (states_hbm, states_ref),
+        (w_hbm.at[0], w_ref.at[:, :w_hbm.shape[2]]), (w_hbm.at[1], w_ref.at[:, w_hbm.shape[2]:]),
         (query_hbm, query_ref), (cot_hbm, cot_ref)))]
+    give = [pltpu.make_async_copy(src, dst, stores.at[at]) for at, (src, dst) in enumerate((
+        (att_ref, att_hbm), (gq_ref, gq_hbm), (gb_ref, gb_hbm), (gkv_ref, gkv_hbm)))]
     for load in fetch:
         load.start()
     dp = lax.axis_index("dp")
@@ -38,8 +42,8 @@
     byte_count = states_ref.shape[1]
     slots = start_ref.shape[2]
     total = nb * slots
-    chunk = w_ref.shape[1]
-    width = w_ref.shape[2]
+    chunk = w_ref.shape[0]
+    width = w_ref.shape[1] // 2
     shared = width // HS
     part = chunk // ng
     group = query_ref.shape[2] // width
@@ -120,6 +124,18 @@
     keys = lax.broadcasted_iota(jnp.int32, (rows, total), 1)
     visible = (keys <= ids) & (jnp.broadcast_to(used, (rows, total)) > 0.5)
 
+    heads = []
+    fetch[4].wait()
+    fetch[5].wait()
+    for c in range(shared):
+        cols = [slice((c * group + h) * HS, (c * group + h + 1) * HS) for h in range(group)]
+        q = jnp.concatenate([query_ref[0, :, at] for at in cols], axis=0)
+        gm = jnp.concatenate([cot_ref[0, :, at] for at in cols], axis=0).astype(F32) * lives
+        heads.append((cols, q, gm, gm.astype(BF16)))
+    fetch[2].wait()
+    fetch[3].wait()
+    wt_ref[...] = w_ref[...].T
+
     for s in range(nb):
         unless(diagonal & (s == b), lambda s=s: remote(
             pooled.at[0, 0], quarter.at[s], s1.at[0], r1.at[s], byte=b).wait_recv())
@@ -130,25 +146,23 @@
     for o in range(1, ng):
         plane_copy(o, g).start()
     pool_all[dp, g] = quarter[...]
-    fetch[2].wait()
     for o in range(1, ng):
         plane_copy(o, lax.rem(g + o, ng)).wait_recv()
 
     for o in range(1, nd):
         remote(pool_all.at[dp], pool_all.at[dp], sd.at[0, o], rd.at[0, dp], dp=lax.rem(dp + o, nd)).start()
 
-    for j in range(2):
-        acc = mm(pool_all[dp, 0].reshape(total, part), w_ref[j, :part], 1, 0)
-        for i in range(1, ng):
-            acc = acc + mm(pool_all[dp, i].reshape(total, part), w_ref[j, i * part:(i + 1) * part], 1, 0)
-        kv_part[:, :, j * width:(j + 1) * width] = acc.astype(BF16).reshape(nb, slots, width)
-    fetch[3].wait()
-    fetch[4].wait()
-
-    def reduce(part, recv, whole, sa, ra, sb, rb):
+    acc = mm(pool_all[dp, 0].reshape(total, part), w_ref[:part], 1, 0)
+    for i in range(1, ng):
+        acc = acc + mm(pool_all[dp, i].reshape(total, part), w_ref[i * part:(i + 1) * part], 1, 0)
+    kv_part[...] = acc.astype(BF16).reshape(nb, slots, 2 * width)
+
+    def reduce(part, recv, whole, sa, ra, sb, rb, beside=None):
         for o in range(1, nb):
             peer = lax.rem(b + o, nb)
             remote(part.at[peer], recv.at[b], sa.at[o], ra.at[b], byte=peer).start()
+        if beside is not None:
+            beside()
         acc = part[b].astype(F32)
         for o in range(1, nb):
             peer = lax.rem(b + o, nb)
@@ -169,13 +183,11 @@
 
     reduce(kv_part, kv_recv, kv_all, s2, r2, s3, r3)
 
+    done = []
     for c in range(shared):
         k = kv_all[:, :, c * HS:(c + 1) * HS].reshape(total, HS)
         v = kv_all[:, :, width + c * HS:width + (c + 1) * HS].reshape(total, HS)
-        cols = [slice((c * group + h) * HS, (c * group + h + 1) * HS) for h in range(group)]
-        q = jnp.concatenate([query_ref[0, :, at] for at in cols], axis=0)
-        gm = jnp.concatenate([cot_ref[0, :, at] for at in cols], axis=0).astype(F32) * lives
-        gm16 = gm.astype(BF16)
+        cols, q, gm, gm16 = heads[c]
         scores = jnp.where(visible, mm(q, k, 1, 1) * factor, -1e30)
         top = jnp.max(scores, axis=1, keepdims=True)
         raised = jnp.where(visible, jnp.exp(scores - top), 0.0)
@@ -187,18 +199,24 @@
         dkv_part[:, :, c * HS:(c + 1) * HS] = mm(ds, q, 0, 0).astype(BF16).reshape(nb, slots, HS)
         dkv_part[:, :, width + c * HS:width + (c + 1) * HS] = (
             mm(pb, gm16, 0, 0).astype(BF16).reshape(nb, slots, HS))
-        att = (mixed * lives).astype(BF16)
-        gq = mm(ds, k, 1, 0).astype(BF16)
-        for h in range(group):
-            att_ref[0, :, cols[h]] = att[h * slots:(h + 1) * slots]
-            gq_ref[0, :, cols[h]] = gq[h * slots:(h + 1) * slots]
-
-    reduce(dkv_part, dkv_recv, dkv_all.at[dp], s4, r4, s5, r5)
+        done.append((cols, mixed, ds, k))
+
+    def outputs():
+        for cols, mixed, ds, k in done:
+            att = (mixed * lives).astype(BF16)
+            gq = mm(ds, k, 1, 0).astype(BF16)
+            for h in range(group):
+                att_ref[0, :, cols[h]] = att[h * slots:(h + 1) * slots]
+                gq_ref[0, :, cols[h]] = gq[h * slots:(h + 1) * slots]
+        give[0].start()
+        give[1].start()
+
+    reduce(dkv_part, dkv_recv, dkv_all.at[dp], s4, r4, s5, r5, outputs)
     for o in range(1, nd):
         remote(dkv_all.at[dp], dkv_all.at[dp], sd.at[1, o], rd.at[1, dp], dp=lax.rem(dp + o, nd)).start()
 
     dkv = dkv_all[dp].reshape(total, 2 * width)
-    terms = mm(dkv[:, :width], w_ref[0], 1, 1) + mm(dkv[:, width:], w_ref[1], 1, 1)
+    terms = mm(dkv, wt_ref[...], 1, 0)
     for i in range(ng):
         dpart[i] = terms[:, i * part:(i + 1) * part].astype(BF16).reshape(nb, slots, part)
 
@@ -214,10 +232,13 @@
         remote(pool_all.at[dp], pool_all.at[other], sd.at[0, o], rd.at[0, other], dp=other).wait_recv()
         remote(dkv_all.at[dp], dkv_all.at[other], sd.at[1, o], rd.at[1, other], dp=other).wait_recv()
     both = dkv_all[...].reshape(nd * total, 2 * width)
-    for i in range(ng):
+    def weights(i):
         product = mm(pool_all[:, i].reshape(nd * total, part), both, 0, 0)
         for j in range(2):
             gkv_ref[j, i * part:(i + 1) * part, :] = product[:, j * width:(j + 1) * width]
+
+    for i in range(ng // 2):
+        weights(i)
 
     acc = dpart[g].astype(F32)
     for o in range(1, ng):
@@ -235,6 +256,10 @@
     @pl.when(diagonal)
     def _():
         drecv[g, piece] = dsum[b]
+
+    for i in range(ng // 2, ng):
+        weights(i)
+    give[3].start()
 
     for g2 in range(ng):
         for c in range(ratio):
@@ -245,6 +270,7 @@
             share = (drecv[i, c].astype(F32) / counts).astype(BF16)
             first_col = c * chunk + i * part
             gb_ref[0, :, first_col:first_col + part] = mm(members, share, 0, 0).astype(BF16)
+    give[2].start()
 
     for g2 in range(ng):
         for c in range(ratio):
@@ -260,6 +286,18 @@
         other = lax.rem(dp + o, nd)
         remote(pool_all.at[dp], pool_all.at[dp], sd.at[0, o], rd.at[0, dp], dp=other).wait_send()
         remote(dkv_all.at[dp], dkv_all.at[dp], sd.at[1, o], rd.at[1, dp], dp=other).wait_send()
+    for store in give:
+        store.wait()
+
+
+def hand_on(*refs):
+    count = len(refs) // 2
+    sems = refs[-1]
+    moves = [pltpu.make_async_copy(refs[at], refs[count + at], sems.at[at]) for at in range(count)]
+    for move in moves:
+        move.start()
+    for move in moves:
+        move.wait()
 
 
 def on_device(nd, ng, nb, byte_states, patch_start, queries, grad_out, w_kv):
@@ -268,8 +306,8 @@
     ratio = nb // ng
     part = chunk // ng
     dma = pltpu.SemaphoreType.DMA
-    vmem = pl.BlockSpec(memory_space=pltpu.VMEM)
-    return pl.pallas_call(
+    hbm = pl.BlockSpec(memory_space=pltpu.HBM)
+    found = pl.pallas_call(
         functools.partial(kernel, nd, ng, nb),
         out_shape=(
             jax.ShapeDtypeStruct(queries.shape, BF16),
@@ -277,15 +315,21 @@
             jax.ShapeDtypeStruct(byte_states.shape, BF16),
             jax.ShapeDtypeStruct(w_kv.shape, F32),
         ),
-        in_specs=[pl.BlockSpec(memory_space=pltpu.HBM)] * 5,
-        out_specs=(vmem,) * 4,
+        in_specs=[hbm] * 5,
+        out_specs=(hbm,) * 4,
         scratch_shapes=[
             pltpu.VMEM(byte_states.shape, BF16),
             pltpu.VMEM(patch_start.shape, patch_start.dtype),
             pltpu.VMEM(queries.shape, BF16),
             pltpu.VMEM(grad_out.shape, BF16),
-            pltpu.VMEM(w_kv.shape, BF16),
-            dma((5,)),
+            pltpu.VMEM((chunk, 2 * width), BF16),
+            pltpu.VMEM((2 * width, chunk), BF16),
+            dma((6,)),
+            pltpu.VMEM(queries.shape, BF16),
+            pltpu.VMEM(queries.shape, BF16),
+            pltpu.VMEM(byte_states.shape, BF16),
+            pltpu.VMEM(w_kv.shape, F32),
+            dma((4,)),
             pltpu.VMEM((ratio, ng, slots, part), BF16),
             pltpu.VMEM((nb, slots, part), BF16),
             pltpu.VMEM((nd, ng, nb, slots, part), BF16),
@@ -305,8 +349,15 @@
             dma((2, nd)), dma((2, nd)),
         ],
         compiler_params=pltpu.CompilerParams(
-            collective_id=0, has_side_effects=True, vmem_limit_bytes=48 * 1024 * 1024),
+            collective_id=0, has_side_effects=True, vmem_limit_bytes=56 * 1024 * 1024),
     )(byte_states, patch_start, queries, grad_out, w_kv)
+    return pl.pallas_call(
+        hand_on,
+        out_shape=tuple(jax.ShapeDtypeStruct(one.shape, one.dtype) for one in found),
+        in_specs=[pl.BlockSpec(memory_space=pl.ANY)] * 4,
+        out_specs=(hbm,) * 4,
+        scratch_shapes=[dma((4,))],
+    )(*found)
 
 
 def solution(mesh):

time: 49.7 us -> 85.7 us (1.72)
  Pallas kernels: 41.6 us -> 84.9 us
  local copies, waits for them, and re-layouts: 7.08 us -> 0 us
    pallas_call x0 -> x1, Pallas kernels: none -> 42.8 us  [on_device(): pl.pallas_call(hand_on, out_shape=tuple((jax.ShapeDtypeStruct(one.shape,...]
    unnamed x14 -> x0, local copies, waits for them, and re-layouts: 7.08 us -> none
where the time goes in v3:
time: 85.7 us; the launch traced here: 85.6 us
  Pallas kernels  84.9 us (99%)
    pallas_call x1, Pallas kernels, on_device(): pl.pallas_call(hand_on, out_shape=tuple((jax.ShapeDtypeStruct(one.shape,...  42.8 us
    pallas_call x1, Pallas kernels, on_device(): pl.pallas_call(functools.partial(kernel, nd, ng, nb), out_shape=(jax.Shap...  42.1 us

profile of v3, /device:TPU:0, one launch (start us, length us, event | category | flops | bytes accessed | tf_op | source)
XLA Modules:
  0.0 85.6 jit_solution(5163529741855843711)
XLA Ops:
  0.6 42.1 %shard_map.84 = (bf16[1,32,512]{2,1,0:T(8,128)(2,1)}, bf16[1,32,512]{2,1,0:T(8,128)(2,1)}, bf16[1,128,1024]{2,1,0:T(8,128)(2,1)}, f32[2,1024,128]{2,1,0:T(8,128)}) custom-call(bf16[1,128,1024]{2,1,0:T(8,128)(2,1)} %states_hbm.1, s32[1,4,32]{2,1,0:T(4,128)} %start_hbm.1, bf16[1,32,512]{2,1,0:T(8,128)(2,1)} %query_hbm.1, bf16[1,32,512]{2,1,0:T(8,128)(2,1)} %cot_hbm.1, ...), custom_call_target="tpu_custom_call" | custom-call | tf_op jit(solution)/shard_map/pallas_call | solution.py:310
  42.7 42.8 %shard_map.85 = (bf16[1,32,512]{2,1,0:T(8,128)(2,1)}, bf16[1,32,512]{2,1,0:T(8,128)(2,1)}, bf16[1,128,1024]{2,1,0:T(8,128)(2,1)}, f32[2,1024,128]{2,1,0:T(8,128)}) custom-call(bf16[1,32,512]{2,1,0:T(8,128)(2,1)} %get-tuple-element.8.refs_0_, bf16[1,32,512]{2,1,0:T(8,128)(2,1)} %get-tuple-element.9.refs_1_, bf16[1,128,1024]{2,1,0:T(8,128)(2,1)} %get-tuple-element.10.refs_2_, ...), custom_call_target="tpu_custom_call" | custom-call | tf_op jit(solution)/shard_map/pallas_call | solution.py:354

commit v4 on v3

--- a/solution.py
+++ b/solution.py
@@ -291,12 +291,21 @@
 
 
 def hand_on(*refs):
-    count = len(refs) // 2
-    sems = refs[-1]
-    moves = [pltpu.make_async_copy(refs[at], refs[count + at], sems.at[at]) for at in range(count)]
-    for move in moves:
+    count = (len(refs) - 2) // 3
+    given, taken, held = refs[:count], refs[count:2 * count], refs[2 * count:3 * count]
+    loads, stores = refs[-2:]
+    inward, outward = [], []
+    for at in range(count):
+        for lead in range(given[at].shape[0]):
+            slot = len(inward)
+            inward.append(pltpu.make_async_copy(given[at].at[lead], held[at].at[lead], loads.at[slot]))
+            outward.append(pltpu.make_async_copy(held[at].at[lead], taken[at].at[lead], stores.at[slot]))
+    for move in inward:
         move.start()
-    for move in moves:
+    for back, move in zip(inward, outward):
+        back.wait()
+        move.start()
+    for move in outward:
         move.wait()
 
 
@@ -356,7 +365,8 @@
         out_shape=tuple(jax.ShapeDtypeStruct(one.shape, one.dtype) for one in found),
         in_specs=[pl.BlockSpec(memory_space=pl.ANY)] * 4,
         out_specs=(hbm,) * 4,
-        scratch_shapes=[dma((4,))],
+        scratch_shapes=[pltpu.VMEM(one.shape, one.dtype) for one in found]
+        + [dma((sum(one.shape[0] for one in found),))] * 2,
     )(*found)
 
 

time: 85.7 us -> 45.1 us (0.53)
  Pallas kernels: 84.9 us -> 44.3 us
    pallas_call x1, Pallas kernels: 42.8 us -> 2.21 us  [on_device(): pl.pallas_call(hand_on, out_shape=tuple((jax.ShapeDtypeStruct(one.shape,...]
where the time goes in v4:
time: 45.1 us; the launch traced here: 45 us
  Pallas kernels  44.3 us (98%)
  between operations  0.64 us (1%)
    pallas_call x1, Pallas kernels, on_device(): pl.pallas_call(functools.partial(kernel, nd, ng, nb), out_shape=(jax.Shap...  42.1 us
    pallas_call x1, Pallas kernels, on_device(): pl.pallas_call(hand_on, out_shape=tuple((jax.ShapeDtypeStruct(one.shape,...  2.21 us

profile of v4, /device:TPU:0, one launch (start us, length us, event | category | flops | bytes accessed | tf_op | source)
XLA Modules:
  0.0 45.0 jit_solution(13356352787644054584)
XLA Ops:
  0.6 42.1 %shard_map.84 = (bf16[1,32,512]{2,1,0:T(8,128)(2,1)}, bf16[1,32,512]{2,1,0:T(8,128)(2,1)}, bf16[1,128,1024]{2,1,0:T(8,128)(2,1)}, f32[2,1024,128]{2,1,0:T(8,128)}) custom-call(bf16[1,128,1024]{2,1,0:T(8,128)(2,1)} %states_hbm.1, s32[1,4,32]{2,1,0:T(4,128)} %start_hbm.1, bf16[1,32,512]{2,1,0:T(8,128)(2,1)} %query_hbm.1, bf16[1,32,512]{2,1,0:T(8,128)(2,1)} %cot_hbm.1, ...), custom_call_target="tpu_custom_call" | custom-call | tf_op jit(solution)/shard_map/pallas_call | solution.py:319
  42.7 2.2 %shard_map.85 = (bf16[1,32,512]{2,1,0:T(8,128)(2,1)}, bf16[1,32,512]{2,1,0:T(8,128)(2,1)}, bf16[1,128,1024]{2,1,0:T(8,128)(2,1)}, f32[2,1024,128]{2,1,0:T(8,128)}) custom-call(bf16[1,32,512]{2,1,0:T(8,128)(2,1)} %get-tuple-element.8.refs_0_, bf16[1,32,512]{2,1,0:T(8,128)(2,1)} %get-tuple-element.9.refs_1_, bf16[1,128,1024]{2,1,0:T(8,128)(2,1)} %get-tuple-element.10.refs_2_, ...), custom_call_target="tpu_custom_call" | custom-call | tf_op jit(solution)/shard_map/pallas_call | solution.py:363

commit v5 on v4

--- a/solution.py
+++ b/solution.py
@@ -136,18 +136,23 @@
     fetch[3].wait()
     wt_ref[...] = w_ref[...].T
 
-    for s in range(nb):
-        unless(diagonal & (s == b), lambda s=s: remote(
-            pooled.at[0, 0], quarter.at[s], s1.at[0], r1.at[s], byte=b).wait_recv())
-
-    def plane_copy(o, slot):
-        return remote(quarter, pool_all.at[dp, slot], s0.at[o], r0.at[slot], glob=lax.rem(g + o, ng))
-
-    for o in range(1, ng):
-        plane_copy(o, g).start()
+    def plane_copy(o, slot, s):
+        return remote(quarter.at[s], pool_all.at[dp, slot, s], s0.at[o, s], r0.at[slot, s],
+                      glob=lax.rem(g + o, ng))
+
+    for k in range(nb):
+        s = lax.rem(b + k, nb)
+
+        def arrive(s=s):
+            remote(pooled.at[0, 0], quarter.at[s], s1.at[0], r1.at[s], byte=b).wait_recv()
+
+        unless(diagonal, arrive) if k == 0 else arrive()
+        for o in range(1, ng):
+            plane_copy(o, g, s).start()
     pool_all[dp, g] = quarter[...]
-    for o in range(1, ng):
-        plane_copy(o, lax.rem(g + o, ng)).wait_recv()
+    for k in range(nb):
+        for o in range(1, ng):
+            plane_copy(o, lax.rem(g + o, ng), lax.rem(b + k, nb)).wait_recv()
 
     for o in range(1, nd):
         remote(pool_all.at[dp], pool_all.at[dp], sd.at[0, o], rd.at[0, dp], dp=lax.rem(dp + o, nd)).start()
@@ -220,12 +225,13 @@
     for i in range(ng):
         dpart[i] = terms[:, i * part:(i + 1) * part].astype(BF16).reshape(nb, slots, part)
 
-    def cut_copy(o, slot):
+    def cut_copy(o, slot, s):
         peer = lax.rem(g + o, ng)
-        return remote(dpart.at[peer], dterm.at[slot], s7.at[o], r7.at[slot], glob=peer)
-
-    for o in range(1, ng):
-        cut_copy(o, g).start()
+        return remote(dpart.at[peer, s], dterm.at[slot, s], s7.at[o, s], r7.at[slot, s], glob=peer)
+
+    for k in range(nb):
+        for o in range(1, ng):
+            cut_copy(o, g, lax.rem(b + k + 1, nb)).start()
 
     for o in range(1, nd):
         other = lax.rem(dp + o, nd)
@@ -240,18 +246,21 @@
     for i in range(ng // 2):
         weights(i)
 
-    acc = dpart[g].astype(F32)
-    for o in range(1, ng):
-        peer = lax.rem(g + o, ng)
-        cut_copy(o, peer).wait_recv()
-        acc = acc + dterm[peer].astype(F32)
-    dsum[...] = acc.astype(BF16)
-
     def patch_copy(s):
-        return remote(dsum.at[s], drecv.at[g, piece], s6.at[s], r6.at[g, piece], glob=owner, byte=jnp.int32(s))
-
-    for s in range(nb):
-        unless(diagonal & (s == b), lambda s=s: patch_copy(s).start())
+        return remote(dsum.at[s], drecv.at[g, piece], s6.at[s], r6.at[g, piece], glob=owner, byte=s)
+
+    for k in range(nb):
+        s = lax.rem(b + k + 1, nb)
+        acc = dpart[g, s].astype(F32)
+        for o in range(1, ng):
+            peer = lax.rem(g + o, ng)
+            cut_copy(o, peer, s).wait_recv()
+            acc = acc + dterm[peer, s].astype(F32)
+        dsum[s] = acc.astype(BF16)
+        if k < nb - 1:
+            patch_copy(s).start()
+        else:
+            unless(diagonal, lambda s=s: patch_copy(s).start())
 
     @pl.when(diagonal)
     def _():
@@ -278,10 +287,11 @@
     sent(kv_part, kv_all, kv_recv, s2, r2, s3, r3)
     sent(dkv_part, dkv_all.at[dp], dkv_recv, s4, r4, s5, r5)
     for o in range(1, ng):
-        plane_copy(o, g).wait_send()
-        cut_copy(o, g).wait_send()
+        for s in range(nb):
+            plane_copy(o, g, s).wait_send()
+            cut_copy(o, g, s).wait_send()
     for s in range(nb):
-        unless(diagonal & (s == b), lambda s=s: patch_copy(s).wait_send())
+        unless(diagonal & (s == b), lambda s=s: patch_copy(jnp.int32(s)).wait_send())
     for o in range(1, nd):
         other = lax.rem(dp + o, nd)
         remote(pool_all.at[dp], pool_all.at[dp], sd.at[0, o], rd.at[0, dp], dp=other).wait_send()
@@ -352,7 +362,7 @@
             pltpu.VMEM((ng, nb, slots, part), BF16),
             pltpu.VMEM((nb, slots, part), BF16),
             pltpu.VMEM((ng, ratio, slots, part), BF16),
-            dma((ng,)), dma((ng,)), dma((ng,)), dma((ng,)),
+            dma((ng, nb)), dma((ng, nb)), dma((ng, nb)), dma((ng, nb)),
             dma((nb,)), dma((nb,)), dma((nb,)), dma((nb,)), dma((nb,)), dma((nb,)),
             dma((nb,)), dma((nb,)), dma((nb,)), dma((nb,)), dma((nb,)), dma((ng, ratio)),
             dma((2, nd)), dma((2, nd)),

time: 45.1 us -> 45.5 us (level)
  no operation moved by 1% of the time
where the time goes in v5:
time: 45.5 us; the launch traced here: 45.4 us
  Pallas kernels  44.7 us (98%)
  between operations  0.64 us (1%)
    pallas_call x1, Pallas kernels, on_device(): pl.pallas_call(functools.partial(kernel, nd, ng, nb), out_shape=(jax.Shap...  42.5 us
    pallas_call x1, Pallas kernels, on_device(): pl.pallas_call(hand_on, out_shape=tuple((jax.ShapeDtypeStruct(one.shape,...  2.21 us

profile of v5, /device:TPU:0, one launch (start us, length us, event | category | flops | bytes accessed | tf_op | source)
XLA Modules:
  0.0 45.4 jit_solution(14826602710309524270)
XLA Ops:
  0.6 42.5 %shard_map.84 = (bf16[1,32,512]{2,1,0:T(8,128)(2,1)}, bf16[1,32,512]{2,1,0:T(8,128)(2,1)}, bf16[1,128,1024]{2,1,0:T(8,128)(2,1)}, f32[2,1024,128]{2,1,0:T(8,128)}) custom-call(bf16[1,128,1024]{2,1,0:T(8,128)(2,1)} %states_hbm.1, s32[1,4,32]{2,1,0:T(4,128)} %start_hbm.1, bf16[1,32,512]{2,1,0:T(8,128)(2,1)} %query_hbm.1, bf16[1,32,512]{2,1,0:T(8,128)(2,1)} %cot_hbm.1, ...), custom_call_target="tpu_custom_call" | custom-call | tf_op jit(solution)/shard_map/pallas_call | solution.py:329
  43.2 2.2 %shard_map.85 = (bf16[1,32,512]{2,1,0:T(8,128)(2,1)}, bf16[1,32,512]{2,1,0:T(8,128)(2,1)}, bf16[1,128,1024]{2,1,0:T(8,128)(2,1)}, f32[2,1024,128]{2,1,0:T(8,128)}) custom-call(bf16[1,32,512]{2,1,0:T(8,128)(2,1)} %get-tuple-element.8.refs_0_, bf16[1,32,512]{2,1,0:T(8,128)(2,1)} %get-tuple-element.9.refs_1_, bf16[1,128,1024]{2,1,0:T(8,128)(2,1)} %get-tuple-element.10.refs_2_, ...), custom_call_target="tpu_custom_call" | custom-call | tf_op jit(solution)/shard_map/pallas_call | solution.py:373
